TPU v7x, 32 devices: a whole 2x2x4 slice. The times are simulated.
32 devices in a mesh: groups: 2 (over y), row: 4 (over z), col: 2 (over x), segment: 2 (over core).
Axes of the slice: x: 2, y: 2, z: 4, core: 2. Of those that a mesh axis runs over, the one named last changes fastest.
Arguments:
- latents: bfloat16 [4, 512, 3072], P(None, ('groups', 'col'), 'row'), parts along dimension 1, may hold values from -6 to 6
- w_in: bfloat16 [2, 3072, 12288], P('segment', 'col', 'row'), may hold values from -0.109375 to 0.109375
- b_in: float32 [2, 12288], P('segment', 'row'), may hold values from -4 to 4
- w_out: bfloat16 [2, 12288, 3072], P('segment', 'row', 'col'), may hold values from -0.0546875 to 0.0546875
- b_out: float32 [2, 3072], P('segment', 'row'), may hold values from -3 to 3
- modulation: float32 [2, 8, 3, 3072], P('segment', 'groups'), parts along dimension 1, may hold values from -3 to 3
Outputs:
- layer_outputs: bfloat16 [2, 4, 512, 3072], P('segment', None, ('groups', 'col'), 'row'), parts along dimension 2
There are 2 independent parts, one for each index of `groups`. A program takes and returns all parts, laid end to end along the dimension named above; an argument that names none is the same for every part. Nothing has to cross between parts.
All inputs are finite; a program needn't handle non-finite values.
Results may differ from a plain program's by a relative error of at most 0.009.
Values may be sent and summed in bfloat16 or wider, within the bound.
A program may use at most 128 MiB of HBM per device.

v0:
```python
import jax
import jax.numpy as jnp
from jax import lax
from jax.sharding import PartitionSpec as P


def shifted(block, axis, distance):
    devices = range(lax.axis_size(axis))
    route = [(i - distance, i) for i in devices if i - distance in devices]
    return lax.ppermute(block, axis, route)


def on_device(latents, w_in, b_in, w_out, b_out, modulation):
    panels = (
        lax.all_gather(w_in, "col", axis=1, tiled=True),
        lax.all_gather(w_out, "col", axis=2, tiled=True),
    )
    w_first = panels[0][0]
    w_second = panels[1][0]
    micro_count = latents.shape[0]
    width = latents.shape[2]
    segment = lax.axis_index("segment")
    segments = lax.axis_size("segment")
    ticks = micro_count + segments - 1
    row_start = lax.axis_index("row") * width
    conditioning = modulation[0]
    bias_first = b_in[0]
    bias_local = b_out[0]
    results = []
    handed = jnp.zeros_like(latents[0])
    for tick in range(ticks):
        if tick > 0:
            handed = shifted(results[-1], "segment", 1)
        first_feed = latents[min(tick, micro_count - 1)]
        feed = jnp.where(segment == 0, first_feed, handed)
        micro = jnp.clip(tick - segment, 0, micro_count - 1)
        mods = lax.dynamic_index_in_dim(conditioning, micro, 0, keepdims=False)
        values = feed.astype(jnp.float32)
        whole = lax.all_gather(feed, "row", axis=1, tiled=True).astype(jnp.float32)
        mean = jnp.mean(whole, axis=-1, keepdims=True)
        var = jnp.mean((whole - mean) ** 2, axis=-1, keepdims=True)
        normed = (whole - mean) * lax.rsqrt(var + 1e-06)
        modulated = (normed * (1.0 + mods[1]) + mods[0]).astype(jnp.bfloat16)
        pre = jnp.dot(modulated, w_first, preferred_element_type=jnp.float32)
        hidden = jax.nn.gelu(pre + bias_first, approximate=True).astype(jnp.bfloat16)
        term = jnp.dot(hidden, w_second, preferred_element_type=jnp.float32)
        branch = lax.psum_scatter(
            term.astype(jnp.bfloat16), "row", scatter_dimension=1, tiled=True
        ).astype(jnp.float32)
        gate_local = lax.dynamic_slice_in_dim(mods[2], row_start, width, 0)
        results.append((values + gate_local * (branch + bias_local)).astype(jnp.bfloat16))
    stacked = jnp.stack(results)
    chosen = lax.dynamic_slice_in_dim(stacked, segment, micro_count, 0)
    return chosen[None]


def solution(mesh):
    return jax.shard_map(
        on_device,
        mesh=mesh,
        in_specs=(
            P(None, ("groups", "col"), "row"),
            P("segment", "col", "row"),
            P("segment", "row"),
            P("segment", "row", "col"),
            P("segment", "row"),
            P("segment", "groups", None, None),
        ),
        out_specs=P("segment", None, ("groups", "col"), "row"),
        check_vma=False,
    )
```

profile of v0, /device:TPU:0, one launch (start us, length us, event | category | flops | bytes accessed | tf_op | source)
XLA Modules:
  0.0 767.9 jit_solution(15648472256520840852)
XLA Ops:
  6.5 0.0 all-gather.4.cloned.1.call-start
  6.5 0.7 all-gather.4.cloned.1.call-update
  7.3 0.0 copy-start
  7.3 0.0 all-gather.6.cloned.1.call-start
  7.3 0.7 all-gather.6.cloned.1.call-update
  8.0 0.0 copy-start.1
  8.0 0.0 reduce-scatter.6.cloned.1.call-start
  8.1 0.3 copy-done
  8.4 0.0 copy-start.3
  8.4 21.3 %all-gather = bf16[1,128,3072]{2,1,0:T(8,128)(2,1)S(1)} all-gather(bf16[1,128,768]{2,1,0:T(8,128)(2,1)S(1)} %slice_select_fusion), channel_id=2, replica_groups=mesh['groups'=2,'row'=4,'col'=2,'segment'=2] {'row'}, dimensions={2}, use_global_device_ids=true | all-gather | bytes 983040 | tf_op jit(solution)/shard_map/all_gather | solution.py:39
  29.7 0.2 convert_reduce_fusion
  29.9 0.4 fusion.77
  30.3 0.0 copy-done.1
  30.3 0.1 dynamic-slice_add_fusion
  30.4 205.6 %all-gather.4.cloned.1.call-done = bf16[1,3072,3072]{2,1,0:T(8,128)(2,1)} async-done(((bf16[1,1536,3072]{2,1,0:T(8,128)(2,1)}), bf16[1,3072,3072]{2,1,0:T(8,128)(2,1)}) %all-gather.4.cloned.1.call-update) | async-done | bytes 18874384 | tf_op jit(solution)/shard_map/all_gather | solution.py:15
  236.0 225.9 %all-gather.6.cloned.1.call-done = bf16[1,3072,3072]{2,1,0:T(8,128)(2,1)} async-done(((bf16[1,3072,1536]{2,1,0:T(8,128)(2,1)}), bf16[1,3072,3072]{2,1,0:T(8,128)(2,1)}) %all-gather.6.cloned.1.call-update) | async-done | bytes 18874384 | tf_op jit(solution)/shard_map/all_gather | solution.py:16
  461.9 0.0 copy-done.3
  461.9 18.4 %fusion.35 = bf16[128,3072]{1,0:T(8,128)(2,1)} fusion(bf16[1,3072,3072]{2,1,0:T(8,128)(2,1)} %all-gather.6.cloned.1.call-done, bf16[1,3072,3072]{2,1,0:T(8,128)(2,1)} %all-gather.4.cloned.1.call-done, bf16[1,128,3072]{2,1,0:T(8,128)(2,1)S(1)} %all-gather, f32[3072]{0:T(1024)S(1)} %bitcast.137, f32[3072]{0:T(1024)S(1)} %bitcast.136, f32[3072]{0:T(1024)S(1)} %bitcast.135, ...), kind=kOutput, calls=%fused_computation.25 | convolution fusion | flops 4838522880 | bytes 39359488 | tf_op jit(solution)/shard_map/dot_general | solution.py:46
  480.3 0.0 reduce-scatter.6.cloned.1.call-update
  480.4 0.0 reduce-scatter.8.cloned.1.call-start
  480.4 0.0 copy-done.2
  480.4 0.1 fusion.193
  480.6 23.2 %reduce-scatter.6.cloned.1.call-done = bf16[128,768]{1,0:T(8,128)(2,1)} async-done(((bf16[128,3072]{1,0:T(8,128)(2,1)}), bf16[128,768]{1,0:T(8,128)(2,1)}) %reduce-scatter.6.cloned.1.call-update) | async-done | bytes 196624 | tf_op jit(solution)/shard_map/reduce_scatter | solution.py:47
  503.8 1.0 bitcast_dynamic-update-slice_fusion.3
  504.8 1.3 collective-permute-start
  506.1 1.0 collective-permute-done
  507.2 18.2 %all_gather.24 = bf16[128,3072]{1,0:T(8,128)(2,1)S(1)} all-gather(bf16[128,768]{1,0:T(8,128)(2,1)S(1)} %bitcast_select_fusion.3), channel_id=1, replica_groups=mesh['groups'=2,'row'=4,'col'=2,'segment'=2] {'row'}, dimensions={1}, use_global_device_ids=true | all-gather | bytes 983040 | tf_op jit(solution)/shard_map/all_gather | solution.py:39
  525.4 0.2 convert_reduce_fusion.4
  525.6 0.4 fusion.70
  526.0 18.4 %fusion.38 = bf16[128,3072]{1,0:T(8,128)(2,1)} fusion(bf16[1,3072,3072]{2,1,0:T(8,128)(2,1)} %all-gather.6.cloned.1.call-done, bf16[1,3072,3072]{2,1,0:T(8,128)(2,1)} %all-gather.4.cloned.1.call-done, bf16[128,3072]{1,0:T(8,128)(2,1)S(1)} %all_gather.24, f32[3072]{0:T(1024)S(1)} %bitcast.134, f32[3072]{0:T(1024)S(1)} %bitcast.133, ...), kind=kOutput, calls=%fused_computation.26 | convolution fusion | flops 4838522880 | bytes 39359488 | tf_op jit(solution)/shard_map/dot_general | solution.py:46
  544.4 0.0 reduce-scatter.8.cloned.1.call-update
  544.4 0.0 reduce-scatter.10.cloned.1.call-start
  544.5 23.1 %reduce-scatter.8.cloned.1.call-done = bf16[128,768]{1,0:T(8,128)(2,1)} async-done(((bf16[128,3072]{1,0:T(8,128)(2,1)}), bf16[128,768]{1,0:T(8,128)(2,1)}) %reduce-scatter.8.cloned.1.call-update) | async-done | bytes 196624 | tf_op jit(solution)/shard_map/reduce_scatter | solution.py:47
  567.6 1.0 bitcast_dynamic-update-slice_fusion.2
  568.6 1.3 collective-permute-start.1
  569.9 1.0 collective-permute-done.1
  571.0 18.3 %all_gather.25 = bf16[128,3072]{1,0:T(8,128)(2,1)S(1)} all-gather(bf16[128,768]{1,0:T(8,128)(2,1)S(1)} %bitcast_select_fusion.2), channel_id=1, replica_groups=mesh['groups'=2,'row'=4,'col'=2,'segment'=2] {'row'}, dimensions={1}, use_global_device_ids=true | all-gather | bytes 983040 | tf_op jit(solution)/shard_map/all_gather | solution.py:39
  589.2 0.2 convert_reduce_fusion.3
  589.4 0.4 fusion.66
  589.8 18.4 %fusion.41 = bf16[128,3072]{1,0:T(8,128)(2,1)} fusion(bf16[1,3072,3072]{2,1,0:T(8,128)(2,1)} %all-gather.6.cloned.1.call-done, bf16[1,3072,3072]{2,1,0:T(8,128)(2,1)} %all-gather.4.cloned.1.call-done, bf16[128,3072]{1,0:T(8,128)(2,1)S(1)} %all_gather.25, f32[3072]{0:T(1024)S(1)} %bitcast.132, f32[3072]{0:T(1024)S(1)} %bitcast.131, ...), kind=kOutput, calls=%fused_computation.27 | convolution fusion | flops 4838522880 | bytes 39359488 | tf_op jit(solution)/shard_map/dot_general | solution.py:46
  608.2 0.0 reduce-scatter.10.cloned.1.call-update
  608.3 0.0 reduce-scatter.12.cloned.1.call-start
  608.3 23.2 %reduce-scatter.10.cloned.1.call-done = bf16[128,768]{1,0:T(8,128)(2,1)} async-done(((bf16[128,3072]{1,0:T(8,128)(2,1)}), bf16[128,768]{1,0:T(8,128)(2,1)}) %reduce-scatter.10.cloned.1.call-update) | async-done | bytes 196624 | tf_op jit(solution)/shard_map/reduce_scatter | solution.py:47
  631.5 1.0 bitcast_dynamic-update-slice_fusion.1
  632.5 1.3 collective-permute-start.2
  633.8 1.0 collective-permute-done.2
  634.9 18.3 %all_gather.26 = bf16[128,3072]{1,0:T(8,128)(2,1)S(1)} all-gather(bf16[128,768]{1,0:T(8,128)(2,1)S(1)} %bitcast_select_fusion.1), channel_id=1, replica_groups=mesh['groups'=2,'row'=4,'col'=2,'segment'=2] {'row'}, dimensions={1}, use_global_device_ids=true | all-gather | bytes 983040 | tf_op jit(solution)/shard_map/all_gather | solution.py:39
  653.2 0.2 convert_reduce_fusion.2
  653.4 0.4 fusion.62
  653.8 18.4 %fusion.44 = bf16[128,3072]{1,0:T(8,128)(2,1)} fusion(bf16[1,3072,3072]{2,1,0:T(8,128)(2,1)} %all-gather.6.cloned.1.call-done, bf16[1,3072,3072]{2,1,0:T(8,128)(2,1)} %all-gather.4.cloned.1.call-done, bf16[128,3072]{1,0:T(8,128)(2,1)S(1)} %all_gather.26, f32[3072]{0:T(1024)S(1)} %bitcast.130, f32[3072]{0:T(1024)S(1)} %bitcast.129, ...), kind=kOutput, calls=%fused_computation.28 | convolution fusion | flops 4838522880 | bytes 39359488 | tf_op jit(solution)/shard_map/dot_general | solution.py:46
  672.2 0.0 reduce-scatter.12.cloned.1.call-update
  672.2 0.0 reduce-scatter.14.cloned.1.call-start
  672.3 23.0 %reduce-scatter.12.cloned.1.call-done = bf16[128,768]{1,0:T(8,128)(2,1)} async-done(((bf16[128,3072]{1,0:T(8,128)(2,1)}), bf16[128,768]{1,0:T(8,128)(2,1)}) %reduce-scatter.12.cloned.1.call-update) | async-done | bytes 196624 | tf_op jit(solution)/shard_map/reduce_scatter | solution.py:47
  695.2 1.0 bitcast_dynamic-update-slice_fusion
  696.3 1.3 collective-permute-start.3
  697.6 1.0 collective-permute-done.3
  698.6 18.4 %all_gather.27 = bf16[128,3072]{1,0:T(8,128)(2,1)S(1)} all-gather(bf16[128,768]{1,0:T(8,128)(2,1)S(1)} %bitcast_select_fusion), channel_id=1, replica_groups=mesh['groups'=2,'row'=4,'col'=2,'segment'=2] {'row'}, dimensions={1}, use_global_device_ids=true | all-gather | bytes 983040 | tf_op jit(solution)/shard_map/all_gather | solution.py:39
  717.0 0.2 convert_reduce_fusion.1
  717.2 0.4 fusion.58
  717.6 18.4 %fusion.47 = bf16[128,3072]{1,0:T(8,128)(2,1)} fusion(bf16[1,3072,3072]{2,1,0:T(8,128)(2,1)} %all-gather.6.cloned.1.call-done, bf16[1,3072,3072]{2,1,0:T(8,128)(2,1)} %all-gather.4.cloned.1.call-done, bf16[128,3072]{1,0:T(8,128)(2,1)S(1)} %all_gather.27, f32[3072]{0:T(1024)S(1)} %bitcast.128, f32[3072]{0:T(1024)S(1)} %bitcast.127, ...), kind=kOutput, calls=%fused_computation.29 | convolution fusion | flops 4838522880 | bytes 39359488 | tf_op jit(solution)/shard_map/dot_general | solution.py:46
  736.0 0.0 reduce-scatter.14.cloned.1.call-update
  736.0 23.0 %reduce-scatter.14.cloned.1.call-done = bf16[128,768]{1,0:T(8,128)(2,1)} async-done(((bf16[128,3072]{1,0:T(8,128)(2,1)}), bf16[128,768]{1,0:T(8,128)(2,1)}) %reduce-scatter.14.cloned.1.call-update) | async-done | bytes 196624 | tf_op jit(solution)/shard_map/reduce_scatter | solution.py:47
  759.1 1.0 fusion.188
  760.1 0.9 dynamic-slice_bitcast_fusion
  (17 shorter events, 0.2 us)
Async XLA Ops:
  6.5 229.5 %all-gather.4.cloned.1.call-start = ((), (), s32[]{:S(2)}) async-start(), calls=%async_computation.5 | async-start | bytes 28311552 | tf_op jit(solution)/shard_map/all_gather | solution.py:15
  7.3 1.1 copy-start
  7.3 454.7 %all-gather.6.cloned.1.call-start = ((), (), s32[]{:S(2)}) async-start(), calls=%async_computation.6 | async-start | bytes 28311552 | tf_op jit(solution)/shard_map/all_gather | solution.py:16
  8.0 22.3 %copy-start.1 = (f32[1,4,3,3072]{3,1,2,0:T(4,128)S(1)}, f32[1,4,3,3072]{3,1,2,0:T(4,128)}, u32[]{:S(2)}) copy-start(f32[1,4,3,3072]{3,1,2,0:T(4,128)} %param.11) | copy-start | bytes 442372
  8.0 495.8 %reduce-scatter.6.cloned.1.call-start = ((), (), s32[]{:S(2)}) async-start(), calls=%async_computation.7 | async-start | bytes 983040 | tf_op jit(solution)/shard_map/reduce_scatter | solution.py:47
  8.4 453.5 %copy-start.3 = (f32[1,3072]{1,0:T(1,128)S(1)}, f32[1,3072]{1,0:T(1,128)}, u32[]{:S(2)}) copy-start(f32[1,3072]{1,0:T(1,128)} %param.8) | copy-start | bytes 36868
  461.9 18.5 %copy-start.2 = (f32[1,768]{1,0:T(1,128)S(1)}, f32[1,768]{1,0:T(1,128)}, u32[]{:S(2)}) copy-start(f32[1,768]{1,0:T(1,128)} %param.10) | copy-start | bytes 9220
  480.4 87.2 %reduce-scatter.8.cloned.1.call-start = ((), (), s32[]{:S(2)}) async-start(), calls=%async_computation.8 | async-start | bytes 983040 | tf_op jit(solution)/shard_map/reduce_scatter | solution.py:47
  504.8 2.4 collective-permute-start
  544.4 87.0 %reduce-scatter.10.cloned.1.call-start = ((), (), s32[]{:S(2)}) async-start(), calls=%async_computation.9 | async-start | bytes 983040 | tf_op jit(solution)/shard_map/reduce_scatter | solution.py:47
  568.6 2.4 collective-permute-start.1
  608.3 87.0 %reduce-scatter.12.cloned.1.call-start = ((), (), s32[]{:S(2)}) async-start(), calls=%async_computation.10 | async-start | bytes 983040 | tf_op jit(solution)/shard_map/reduce_scatter | solution.py:47
  632.5 2.4 collective-permute-start.2
  672.2 86.8 %reduce-scatter.14.cloned.1.call-start = ((), (), s32[]{:S(2)}) async-start(), calls=%async_computation.11 | async-start | bytes 983040 | tf_op jit(solution)/shard_map/reduce_scatter | solution.py:47
  696.3 2.4 collective-permute-start.3
Sparse Core Ops, SparseCore 0:
  8.9 227.0 all-gather.3
  237.6 224.3 all-gather.5
  480.5 23.2 reduce-scatter.5
  544.6 22.9 reduce-scatter.7
  608.4 23.0 reduce-scatter.9
  672.3 22.8 reduce-scatter.11
  736.2 22.8 reduce-scatter.13
where the time goes:
time: 768 us
  waiting for transfers between devices  553 us (72%)
  blocking collectives  94.5 us (12%)
  matrix products  92.1 us (12%)
  between operations  13.6 us (2%)
  other arithmetic  8.14 us (1%)
    all_gather x1, waiting for transfers between devices, on_device(): lax.all_gather(w_out, 'col', axis=2, tiled=True)  226 us
    all_gather x1, waiting for transfers between devices, on_device(): lax.all_gather(w_in, 'col', axis=1, tiled=True)  206 us
    reduce_scatter x5, waiting for transfers between devices, on_device(): lax.psum_scatter(term.astype(jnp.bfloat16), 'row', scatter_dimension=1, t...  115 us
    all_gather x5, blocking collectives, on_device(): whole = lax.all_gather(feed, 'row', axis=1, tiled=True).astype(jnp.float32)  94.5 us
    dot_general x5, matrix products, on_device(): term = jnp.dot(hidden, w_second, preferred_element_type=jnp.float32)  92.1 us
  transfers between devices with their start and end apart: 11, of which 11 were waited for; matrix products, arithmetic and copies ran while one was open for 0% of the time, Pallas kernels for 0%

commit v1 on v0

--- a/solution.py
+++ b/solution.py
@@ -2,6 +2,34 @@
 import jax.numpy as jnp
 from jax import lax
 from jax.sharding import PartitionSpec as P
+
+
+def _move_tasks(t0, dim_i):
+    u_next = list(t0.shape[1:])
+    u_next[dim_i] *= t0.shape[0]
+    h_now = jnp.moveaxis(t0, 0, dim_i).reshape(u_next)
+    return h_now
+
+
+def work_samples(content, dev_axis):
+    q_n = lax.axis_size(dev_axis)
+    current_block = content[None]
+    for dd in range(q_n.bit_length() - 1):
+        low = 1 << dd
+        frame_out = lax.ppermute(
+            current_block,
+            axis_name=dev_axis,
+            perm=list(map(lambda dev_i: (dev_i, dev_i ^ low), range(q_n))),
+        )
+        z_new = jnp.stack([current_block, frame_out])
+        passed = lax.axis_index(dev_axis) >> dd & 1
+        current_block = jnp.where(passed == 0, z_new, z_new[::-1]).reshape(-1, *content.shape)
+    return current_block
+
+
+def stacks_all_hold(body, my_data, d_out):
+    work_now = _move_tasks(work_samples(body, my_data), d_out)
+    return work_now
 
 
 def shifted(block, axis, distance):
@@ -11,10 +39,7 @@
 
 
 def on_device(latents, w_in, b_in, w_out, b_out, modulation):
-    panels = (
-        lax.all_gather(w_in, "col", axis=1, tiled=True),
-        lax.all_gather(w_out, "col", axis=2, tiled=True),
-    )
+    panels = (stacks_all_hold(w_in, "col", 1), lax.all_gather(w_out, "col", axis=2, tiled=True))
     w_first = panels[0][0]
     w_second = panels[1][0]
     micro_count = latents.shape[0]

time: 768 us -> 724 us (0.943)
  waiting for transfers between devices: 553 us -> 488 us
  other arithmetic: 8.14 us -> 27.1 us
    ppermute x0 -> x1, waiting for transfers between devices: none -> 364 us  [work_samples(): lax.ppermute(current_block, axis_name=dev_axis, perm=list(map(lambda dev_...]
    all_gather x1, waiting for transfers between devices: 226 us -> 1.76 us  [on_device(): lax.all_gather(w_out, 'col', axis=2, tiled=True)]
    all_gather x1 -> x0, waiting for transfers between devices: 206 us -> none  [on_device(): lax.all_gather(w_in, 'col', axis=1, tiled=True)]
    select_n x0 -> x1, other arithmetic: none -> 9.75 us  [work_samples(): jnp.where(passed == 0, z_new, z_new[::-1]).reshape(-1, *content.shape)]
    another operation x0 -> x1, other arithmetic: none -> 9.19 us  [work_samples(): z_new = jnp.stack([current_block, frame_out])]
  transfers between devices with their start and end apart: 11 -> 11, of which waited for: 11 -> 11; matrix products, arithmetic and copies ran while one was open for 0% -> 3% of each run, Pallas kernels for 0% -> 0%
where the time goes in v1:
time: 724 us; the launch traced here: 723 us
  waiting for transfers between devices  488 us (67%)
  blocking collectives  93.2 us (13%)
  matrix products  92.1 us (13%)
  other arithmetic  27.1 us (4%)
  between operations  13.6 us (2%)
  starting transfers between devices  8.42 us (1%)
    ppermute x1, waiting for transfers between devices, work_samples(): lax.ppermute(current_block, axis_name=dev_axis, perm=list(map(lambda dev_...  364 us
    reduce_scatter x5, waiting for transfers between devices, on_device(): lax.psum_scatter(term.astype(jnp.bfloat16), 'row', scatter_dimension=1, t...  117 us
    all_gather x5, blocking collectives, on_device(): whole = lax.all_gather(feed, 'row', axis=1, tiled=True).astype(jnp.float32)  93.2 us
    dot_general x5, matrix products, on_device(): term = jnp.dot(hidden, w_second, preferred_element_type=jnp.float32)  92.1 us
  transfers between devices with their start and end apart: 11, of which 11 were waited for; matrix products, arithmetic and copies ran while one was open for 3% of the time, Pallas kernels for 0%

profile of v1, /device:TPU:0, one launch (start us, length us, event | category | flops | bytes accessed | tf_op | source)
XLA Modules:
  0.0 723.3 jit_solution(3159794816178448700)
XLA Ops:
  6.5 0.0 all-gather.3.cloned.1.call-start
  6.5 0.7 all-gather.3.cloned.1.call-update
  7.3 0.0 copy-start.1
  7.3 0.0 reduce-scatter.6.cloned.1.call-start
  7.3 3.0 collective-permute-start
  10.3 0.0 copy-done
  10.3 19.9 %all-gather = bf16[1,128,3072]{2,1,0:T(8,128)(2,1)S(1)} all-gather(bf16[1,128,768]{2,1,0:T(8,128)(2,1)S(1)} %slice_select_fusion), channel_id=2, replica_groups=mesh['groups'=2,'row'=4,'col'=2,'segment'=2] {'row'}, dimensions={2}, use_global_device_ids=true | all-gather | bytes 983040 | tf_op jit(solution)/shard_map/all_gather | solution.py:64
  30.3 0.2 convert_reduce_fusion
  30.5 0.4 fusion.52
  30.8 0.0 copy-done.1
  30.8 0.1 dynamic-slice_add_fusion
  31.0 364.2 %collective-permute-done = bf16[1,1,1536,3072]{3,2,1,0:T(8,128)(2,1)} collective-permute-done((bf16[1,1,1536,3072]{3,2,1,0:T(8,128)(2,1)}, bf16[1,1,1536,3072]{3,2,1,0:T(8,128)(2,1)}, u32[]{:S(2)}, u32[]{:S(2)}) %collective-permute-start) | collective-permute-done | bytes 9437216 | tf_op jit(solution)/shard_map/ppermute | solution.py:19
  395.2 9.2 %pad_maximum_fusion = bf16[2,1,1,1536,3072]{4,3,2,1,0:T(8,128)(2,1)S(1)} fusion(bf16[1,1,1,1536,3072]{4,3,2,1,0:T(8,128)(2,1)} %bitcast.6, bf16[1,1,1,1536,3072]{4,3,2,1,0:T(8,128)(2,1)} %bitcast.91), kind=kLoop, calls=%fused_computation.1 | loop fusion | flops 9437184 | bytes 37748736 | tf_op jit(solution)/shard_map/stack | solution.py:24
  404.4 0.0 copy-start.3
  404.4 9.7 %reverse_select_fusion = bf16[2,1,1,1536,3072]{4,3,2,1,0:T(8,128)(2,1)} fusion(bf16[2,1,1,1536,3072]{4,3,2,1,0:T(8,128)(2,1)S(1)} %pad_maximum_fusion, pred[]{:T(512)S(6)} %eq.5), kind=kLoop, calls=%fused_computation | loop fusion | flops 9437184 | bytes 37748736 | tf_op jit(solution)/shard_map/jit(_where)/select_n | solution.py:26
  414.2 1.8 all-gather.3.cloned.1.call-done
  415.9 0.0 copy-done.3
  415.9 18.4 %fusion.10 = bf16[128,3072]{1,0:T(8,128)(2,1)} fusion(bf16[1,3072,3072]{2,1,0:T(8,128)(2,1)} %all-gather.3.cloned.1.call-done, bf16[3072,3072]{1,0:T(8,128)(2,1)} %bitcast.85, bf16[1,128,3072]{2,1,0:T(8,128)(2,1)S(1)} %all-gather, f32[3072]{0:T(1024)S(1)} %bitcast.102, f32[3072]{0:T(1024)S(1)} %bitcast.101, f32[3072]{0:T(1024)S(1)} %bitcast.100, ...), kind=kOutput, calls=%fused_computation.17 | convolution fusion | flops 4838522880 | bytes 39359488 | tf_op jit(solution)/shard_map/dot_general | solution.py:71
  434.4 0.0 reduce-scatter.6.cloned.1.call-update
  434.4 0.0 reduce-scatter.8.cloned.1.call-start
  434.4 0.0 copy-done.2
  434.5 0.1 fusion.138
  434.6 24.7 %reduce-scatter.6.cloned.1.call-done = bf16[128,768]{1,0:T(8,128)(2,1)} async-done(((bf16[128,3072]{1,0:T(8,128)(2,1)}), bf16[128,768]{1,0:T(8,128)(2,1)}) %reduce-scatter.6.cloned.1.call-update) | async-done | bytes 196624 | tf_op jit(solution)/shard_map/reduce_scatter | solution.py:72
  459.3 1.0 bitcast_dynamic-update-slice_fusion.3
  460.3 1.3 collective-permute-start.1
  461.6 1.0 collective-permute-done.1
  462.7 18.3 %all_gather.20 = bf16[128,3072]{1,0:T(8,128)(2,1)S(1)} all-gather(bf16[128,768]{1,0:T(8,128)(2,1)S(1)} %bitcast_select_fusion.3), channel_id=1, replica_groups=mesh['groups'=2,'row'=4,'col'=2,'segment'=2] {'row'}, dimensions={1}, use_global_device_ids=true | all-gather | bytes 983040 | tf_op jit(solution)/shard_map/all_gather | solution.py:64
  481.0 0.2 convert_reduce_fusion.4
  481.2 0.4 fusion.45
  481.6 18.4 %fusion.13 = bf16[128,3072]{1,0:T(8,128)(2,1)} fusion(bf16[1,3072,3072]{2,1,0:T(8,128)(2,1)} %all-gather.3.cloned.1.call-done, bf16[3072,3072]{1,0:T(8,128)(2,1)} %bitcast.86, bf16[128,3072]{1,0:T(8,128)(2,1)S(1)} %all_gather.20, f32[3072]{0:T(1024)S(1)} %bitcast.99, f32[3072]{0:T(1024)S(1)} %bitcast.98, f32[128]{0:T(128)S(1)} %add_rsqrt_fusion.3, ...), kind=kOutput, calls=%fused_computation.18 | convolution fusion | flops 4838522880 | bytes 39359488 | tf_op jit(solution)/shard_map/dot_general | solution.py:71
  500.0 0.0 reduce-scatter.8.cloned.1.call-update
  500.0 0.0 reduce-scatter.10.cloned.1.call-start
  500.1 23.1 %reduce-scatter.8.cloned.1.call-done = bf16[128,768]{1,0:T(8,128)(2,1)} async-done(((bf16[128,3072]{1,0:T(8,128)(2,1)}), bf16[128,768]{1,0:T(8,128)(2,1)}) %reduce-scatter.8.cloned.1.call-update) | async-done | bytes 196624 | tf_op jit(solution)/shard_map/reduce_scatter | solution.py:72
  523.2 1.0 bitcast_dynamic-update-slice_fusion.2
  524.2 1.3 collective-permute-start.2
  525.5 1.0 collective-permute-done.2
  526.5 18.3 %all_gather.21 = bf16[128,3072]{1,0:T(8,128)(2,1)S(1)} all-gather(bf16[128,768]{1,0:T(8,128)(2,1)S(1)} %bitcast_select_fusion.2), channel_id=1, replica_groups=mesh['groups'=2,'row'=4,'col'=2,'segment'=2] {'row'}, dimensions={1}, use_global_device_ids=true | all-gather | bytes 983040 | tf_op jit(solution)/shard_map/all_gather | solution.py:64
  544.9 0.2 convert_reduce_fusion.3
  545.1 0.4 fusion.41
  545.4 18.4 %fusion.16 = bf16[128,3072]{1,0:T(8,128)(2,1)} fusion(bf16[1,3072,3072]{2,1,0:T(8,128)(2,1)} %all-gather.3.cloned.1.call-done, bf16[3072,3072]{1,0:T(8,128)(2,1)} %bitcast.87, bf16[128,3072]{1,0:T(8,128)(2,1)S(1)} %all_gather.21, f32[3072]{0:T(1024)S(1)} %bitcast.97, f32[3072]{0:T(1024)S(1)} %bitcast.96, f32[128]{0:T(128)S(1)} %add_rsqrt_fusion.2, ...), kind=kOutput, calls=%fused_computation.19 | convolution fusion | flops 4838522880 | bytes 39359488 | tf_op jit(solution)/shard_map/dot_general | solution.py:71
  563.9 0.0 reduce-scatter.10.cloned.1.call-update
  563.9 0.0 reduce-scatter.12.cloned.1.call-start
  564.0 23.0 %reduce-scatter.10.cloned.1.call-done = bf16[128,768]{1,0:T(8,128)(2,1)} async-done(((bf16[128,3072]{1,0:T(8,128)(2,1)}), bf16[128,768]{1,0:T(8,128)(2,1)}) %reduce-scatter.10.cloned.1.call-update) | async-done | bytes 196624 | tf_op jit(solution)/shard_map/reduce_scatter | solution.py:72
  587.0 1.0 bitcast_dynamic-update-slice_fusion.1
  588.0 1.3 collective-permute-start.3
  589.3 1.0 collective-permute-done.3
  590.3 18.3 %all_gather.22 = bf16[128,3072]{1,0:T(8,128)(2,1)S(1)} all-gather(bf16[128,768]{1,0:T(8,128)(2,1)S(1)} %bitcast_select_fusion.1), channel_id=1, replica_groups=mesh['groups'=2,'row'=4,'col'=2,'segment'=2] {'row'}, dimensions={1}, use_global_device_ids=true | all-gather | bytes 983040 | tf_op jit(solution)/shard_map/all_gather | solution.py:64
  608.6 0.2 convert_reduce_fusion.2
  608.8 0.4 fusion.37
  609.2 18.4 %fusion.19 = bf16[128,3072]{1,0:T(8,128)(2,1)} fusion(bf16[1,3072,3072]{2,1,0:T(8,128)(2,1)} %all-gather.3.cloned.1.call-done, bf16[3072,3072]{1,0:T(8,128)(2,1)} %bitcast.88, bf16[128,3072]{1,0:T(8,128)(2,1)S(1)} %all_gather.22, f32[3072]{0:T(1024)S(1)} %bitcast.95, f32[3072]{0:T(1024)S(1)} %bitcast.94, f32[128]{0:T(128)S(1)} %add_rsqrt_fusion.1, ...), kind=kOutput, calls=%fused_computation.20 | convolution fusion | flops 4838522880 | bytes 39359488 | tf_op jit(solution)/shard_map/dot_general | solution.py:71
  627.6 0.0 reduce-scatter.12.cloned.1.call-update
  627.7 0.0 reduce-scatter.14.cloned.1.call-start
  627.7 23.0 %reduce-scatter.12.cloned.1.call-done = bf16[128,768]{1,0:T(8,128)(2,1)} async-done(((bf16[128,3072]{1,0:T(8,128)(2,1)}), bf16[128,768]{1,0:T(8,128)(2,1)}) %reduce-scatter.12.cloned.1.call-update) | async-done | bytes 196624 | tf_op jit(solution)/shard_map/reduce_scatter | solution.py:72
  650.7 1.0 bitcast_dynamic-update-slice_fusion
  651.7 1.3 collective-permute-start.4
  653.0 1.0 collective-permute-done.4
  654.1 18.4 %all_gather.23 = bf16[128,3072]{1,0:T(8,128)(2,1)S(1)} all-gather(bf16[128,768]{1,0:T(8,128)(2,1)S(1)} %bitcast_select_fusion), channel_id=1, replica_groups=mesh['groups'=2,'row'=4,'col'=2,'segment'=2] {'row'}, dimensions={1}, use_global_device_ids=true | all-gather | bytes 983040 | tf_op jit(solution)/shard_map/all_gather | solution.py:64
  672.5 0.2 convert_reduce_fusion.1
  672.7 0.4 fusion.33
  673.0 18.4 %fusion.22 = bf16[128,3072]{1,0:T(8,128)(2,1)} fusion(bf16[1,3072,3072]{2,1,0:T(8,128)(2,1)} %all-gather.3.cloned.1.call-done, bf16[3072,3072]{1,0:T(8,128)(2,1)} %bitcast.89, bf16[128,3072]{1,0:T(8,128)(2,1)S(1)} %all_gather.23, f32[3072]{0:T(1024)S(1)} %bitcast.93, f32[3072]{0:T(1024)S(1)} %bitcast.92, f32[128]{0:T(128)S(1)} %add_rsqrt_fusion, ...), kind=kOutput, calls=%fused_computation.21 | convolution fusion | flops 4838522880 | bytes 39359488 | tf_op jit(solution)/shard_map/dot_general | solution.py:71
  691.4 0.0 reduce-scatter.14.cloned.1.call-update
  691.5 23.1 %reduce-scatter.14.cloned.1.call-done = bf16[128,768]{1,0:T(8,128)(2,1)} async-done(((bf16[128,3072]{1,0:T(8,128)(2,1)}), bf16[128,768]{1,0:T(8,128)(2,1)}) %reduce-scatter.14.cloned.1.call-update) | async-done | bytes 196624 | tf_op jit(solution)/shard_map/reduce_scatter | solution.py:72
  714.5 1.0 fusion.133
  715.5 0.9 dynamic-slice_bitcast_fusion
  (18 shorter events, 0.2 us)
Async XLA Ops:
  6.5 3.8 copy-start
  6.5 409.4 %all-gather.3.cloned.1.call-start = ((), (), s32[]{:S(2)}) async-start(), calls=%async_computation.5 | async-start | bytes 28311552 | tf_op jit(solution)/shard_map/all_gather | solution.py:42
  7.3 23.6 %copy-start.1 = (f32[1,4,3,3072]{3,1,2,0:T(4,128)S(1)}, f32[1,4,3,3072]{3,1,2,0:T(4,128)}, u32[]{:S(2)}) copy-start(f32[1,4,3,3072]{3,1,2,0:T(4,128)} %param.11) | copy-start | bytes 442372
  7.3 452.0 %reduce-scatter.6.cloned.1.call-start = ((), (), s32[]{:S(2)}) async-start(), calls=%async_computation.6 | async-start | bytes 983040 | tf_op jit(solution)/shard_map/reduce_scatter | solution.py:72
  7.3 387.9 %collective-permute-start = (bf16[1,1,1536,3072]{3,2,1,0:T(8,128)(2,1)}, bf16[1,1,1536,3072]{3,2,1,0:T(8,128)(2,1)}, u32[]{:S(2)}, u32[]{:S(2)}) collective-permute-start(bf16[1,1,1536,3072]{3,2,1,0:T(8,128)(2,1)} %bitcast.90), channel_id=1, source_target_pairs={{0,2},{2,0},{1,3},{3,1},{4,6},{6,4},{5,7},{7,5},{8,10},{10,8},{9,1... | collective-permute-start | bytes 28311560 | tf_op jit(solution)/shard_map/ppermute | solution.py:19
  404.4 11.5 %copy-start.3 = (f32[1,3072]{1,0:T(1,128)S(1)}, f32[1,3072]{1,0:T(1,128)}, u32[]{:S(2)}) copy-start(f32[1,3072]{1,0:T(1,128)} %param.8) | copy-start | bytes 36868
  415.9 18.5 %copy-start.2 = (f32[1,768]{1,0:T(1,128)S(1)}, f32[1,768]{1,0:T(1,128)}, u32[]{:S(2)}) copy-start(f32[1,768]{1,0:T(1,128)} %param.10) | copy-start | bytes 9220
  434.4 88.8 %reduce-scatter.8.cloned.1.call-start = ((), (), s32[]{:S(2)}) async-start(), calls=%async_computation.7 | async-start | bytes 983040 | tf_op jit(solution)/shard_map/reduce_scatter | solution.py:72
  460.3 2.4 collective-permute-start.1
  500.0 86.9 %reduce-scatter.10.cloned.1.call-start = ((), (), s32[]{:S(2)}) async-start(), calls=%async_computation.8 | async-start | bytes 983040 | tf_op jit(solution)/shard_map/reduce_scatter | solution.py:72
  524.2 2.4 collective-permute-start.2
  563.9 86.8 %reduce-scatter.12.cloned.1.call-start = ((), (), s32[]{:S(2)}) async-start(), calls=%async_computation.9 | async-start | bytes 983040 | tf_op jit(solution)/shard_map/reduce_scatter | solution.py:72
  588.0 2.4 collective-permute-start.3
  627.7 86.9 %reduce-scatter.14.cloned.1.call-start = ((), (), s32[]{:S(2)}) async-start(), calls=%async_computation.10 | async-start | bytes 983040 | tf_op jit(solution)/shard_map/reduce_scatter | solution.py:72
  651.7 2.4 collective-permute-start.4
Sparse Core Ops, SparseCore 0:
  8.9 406.9 all-gather.2
  434.5 24.7 reduce-scatter.5
  500.1 22.9 reduce-scatter.7
  564.0 22.8 reduce-scatter.9
  627.8 22.8 reduce-scatter.11
  691.6 22.8 reduce-scatter.13
